TPU v7x, 512 devices: a whole 4x4x16 slice. The times are simulated.
512 devices in a mesh: rows: 32 (over z, core), vocab: 16 (over x, y).
Axes of the slice: x: 4, y: 4, z: 16, core: 2. Of those that a mesh axis runs over, the one named last changes fastest.
Arguments:
- student_hidden: bfloat16 [192, 5120], P('rows', 'vocab'), may hold values from -12 to 12
- teacher_hidden: bfloat16 [192, 4096], P('rows', 'vocab'), may hold values from -12 to 12
- student_head: bfloat16 [5120, 143360], P(None, ('rows', 'vocab')), may hold values from -0.13975425 to 0.13975425
- teacher_head: bfloat16 [4096, 143360], P(None, ('rows', 'vocab')), may hold values from -0.15625 to 0.15625
- teacher_row: int32 [192], replicated, may hold values from 0 to 191, each once
- live_counts: int32 [32], replicated, may hold values from 1 to 6, 112 in all
- branch_id: int32 [192], replicated, may hold values from 0 to 15
- branch_ratio: float32 [16], replicated, may hold values from 0.25 to 4
Outputs:
- token_loss: float32 [192], P('rows')
- grad_hidden: float32 [192, 5120], P('rows', 'vocab')
Inputs may be any that keep to these rules, and one draw needn't show every extreme that they name: `live_counts`: the counts sum to 112.
All inputs are finite; a program needn't handle non-finite values.
Results may differ from a plain program's by a relative error of at most 0.0045.
Values may be sent and summed in bfloat16 or wider, within the bound.
A program may use at most 64 MiB of HBM per device.

v0:
```python
import jax
import jax.numpy as jnp
from jax import lax
from jax.sharding import PartitionSpec as P


def head_product(block, head):
    return lax.dot_general(
        block, head, (((1,), (1,)), ((), ())), preferred_element_type=jnp.float32
    )


def on_device(
    student_hidden,
    teacher_hidden,
    student_head,
    teacher_head,
    teacher_row,
    live_counts,
    branch_id,
    branch_ratio,
):
    rows_here = student_hidden.shape[0]
    feat_width = student_hidden.shape[1]
    student_feat, teacher_feat = (
        lax.all_gather(student_hidden, "vocab", axis=1, tiled=True),
        lax.all_gather(teacher_hidden, "vocab", axis=1, tiled=True),
    )
    student_logits = jnp.dot(
        lax.all_gather(student_feat, "rows", axis=0, tiled=True),
        student_head,
        preferred_element_type=jnp.float32,
    )
    teacher_ordered = jnp.dot(
        lax.all_gather(teacher_feat, "rows", axis=0, tiled=True),
        teacher_head,
        preferred_element_type=jnp.float32,
    )
    teacher_logits = jnp.take(teacher_ordered, teacher_row, axis=0)
    logit_diff = student_logits - teacher_logits
    peak_s, peak_t = lax.pmax(
        (jnp.max(student_logits, axis=1), jnp.max(teacher_logits, axis=1)), ("rows", "vocab")
    )
    expo_s = jnp.exp(student_logits - peak_s[:, None])
    expo_t = jnp.exp(teacher_logits - peak_t[:, None])
    sum_s, sum_t, cross = lax.psum(
        (jnp.sum(expo_s, axis=1), jnp.sum(expo_t, axis=1), jnp.sum(expo_s * logit_diff, axis=1)),
        ("rows", "vocab"),
    )
    lse_s = peak_s + jnp.log(sum_s)
    lse_t = peak_t + jnp.log(sum_t)
    divergence = cross / sum_s - lse_s + lse_t
    tokens_all = student_logits.shape[0]
    position = jnp.arange(tokens_all, dtype=jnp.int32)
    owners = live_counts.shape[0]
    owner_ids = jnp.arange(owners, dtype=jnp.int32)
    owner_match = (position // rows_here)[:, None] == owner_ids[None, :]
    owner_live = jnp.sum(jnp.where(owner_match, live_counts[None, :], 0), axis=1)
    live = (position % rows_here < owner_live).astype(jnp.float32)
    branches = branch_ratio.shape[0]
    branch_match = branch_id[:, None] == jnp.arange(branches, dtype=jnp.int32)[None, :]
    ratio = jnp.sum(jnp.where(branch_match, branch_ratio[None, :], 0.0), axis=1)
    weight = live * ratio
    all_loss = weight * divergence
    student_logp = student_logits - lse_s[:, None]
    log_gap = student_logp - (teacher_logits - lse_t[:, None])
    logit_grad = (weight[:, None] * jnp.exp(student_logp) * (log_gap - divergence[:, None])).astype(
        jnp.bfloat16
    )
    row_index = lax.axis_index("rows")
    token_loss = lax.dynamic_slice_in_dim(all_loss, row_index * rows_here, rows_here, 0)
    partial_grad = head_product(logit_grad, student_head)
    total_grad = lax.psum(partial_grad, ("rows", "vocab"))
    feat_index = lax.axis_index("vocab")
    grad_hidden = lax.dynamic_slice(
        total_grad, (row_index * rows_here, feat_index * feat_width), (rows_here, feat_width)
    )
    return (token_loss, grad_hidden)


def solution(mesh):
    in_specs = (
        P("rows", "vocab"),
        P("rows", "vocab"),
        P(None, ("rows", "vocab")),
        P(None, ("rows", "vocab")),
        P(),
        P(),
        P(),
        P(),
    )
    out_specs = (P("rows"), P("rows", "vocab"))
    return jax.shard_map(
        on_device, mesh=mesh, in_specs=in_specs, out_specs=out_specs, check_vma=False
    )
```

profile of v0, /device:TPU:1, one launch (start us, length us, event | category | flops | bytes accessed | tf_op | source)
XLA Modules:
  0.0 980.8 jit_solution(7937474398704583633)
XLA Ops:
  7.2 0.0 copy-start
  7.2 0.0 all-gather.8.cloned.1.call-start
  7.2 22.0 %all_gather.14 = bf16[6,4096]{1,0:T(8,128)(2,1)} all-gather(bf16[6,256]{1,0:T(8,128)(2,1)} %param.9), channel_id=1, replica_groups=mesh['rows'=32,'vocab'=16] {'vocab'}, dimensions={1}, use_global_device_ids=true | all-gather | bytes 52224 | tf_op jit(solution)/shard_map/all_gather | solution.py:27
  29.2 0.0 all-gather.8.cloned.1.call-update
  29.2 0.0 all-gather.6.cloned.1.call-start
  29.3 17.1 %all-gather = bf16[16,320,6]{1,2,0:T(8,128)(2,1)S(1)} all-gather(bf16[1,320,6]{1,2,0:T(8,128)(2,1)} %bitcast.16), channel_id=1, replica_groups=mesh['rows'=32,'vocab'=16] {'vocab'}, dimensions={0}, use_global_device_ids=true | all-gather | bytes 65280 | tf_op jit(solution)/shard_map/all_gather | solution.py:26
  46.4 0.8 reshape.52
  47.1 0.0 all-gather.6.cloned.1.call-update
  47.2 0.0 all-reduce.3.cloned.1.call-start
  47.2 0.7 compare_select_fusion
  47.9 0.7 select_reduce_fusion.1
  48.7 0.8 select_reduce_fusion.2
  49.5 0.7 compare_and_fusion
  50.1 58.3 %all-gather.8.cloned.1.call-done = bf16[32,6,4096]{2,1,0:T(8,128)(2,1)} async-done(((bf16[1,6,4096]{2,1,0:T(8,128)(2,1)}), bf16[32,6,4096]{2,1,0:T(8,128)(2,1)}) %all-gather.8.cloned.1.call-update) | async-done | bytes 1572880 | tf_op jit(solution)/shard_map/all_gather | solution.py:35
  108.5 3.7 reshape.56
  112.1 3.3 fusion.12
  115.5 0.9 gather_fusion
  116.3 0.1 copy.20
  116.5 63.6 %all-gather.6.cloned.1.call-done = bf16[32,6,5120]{2,1,0:T(8,128)(2,1)} async-done(((bf16[1,6,5120]{2,1,0:T(8,128)(2,1)}), bf16[32,6,5120]{2,1,0:T(8,128)(2,1)}) %all-gather.6.cloned.1.call-update) | async-done | bytes 1966096 | tf_op jit(solution)/shard_map/all_gather | solution.py:30
  180.1 4.1 reshape.54
  184.2 0.0 copy-done
  184.2 2.5 fusion.11
  186.7 102.9 %pmax.14 = f32[192]{0:T(256)S(1)} all-reduce(f32[192]{0:T(256)S(1)} %get-tuple-element.13), channel_id=1, replica_groups=mesh['rows'=32,'vocab'=16] {'rows','vocab'}, use_global_device_ids=true, to_apply=%region_3.4 | all-reduce | flops 192 | bytes 1536 | tf_op jit(solution)/shard_map/pmax | solution.py:41
  289.6 0.1 multiply_reduce_fusion
  289.8 98.4 %pmax.15 = f32[192]{0:T(256)S(1)} all-reduce(f32[192]{0:T(256)S(1)} %get-tuple-element.4), channel_id=1, replica_groups=mesh['rows'=32,'vocab'=16] {'rows','vocab'}, use_global_device_ids=true, to_apply=%region_9.10 | all-reduce | flops 192 | bytes 1536 | tf_op jit(solution)/shard_map/pmax | solution.py:41
  388.1 0.1 exponential_reduce_fusion
  388.2 100.1 %all-reduce = (f32[192]{0:T(256)S(1)}, f32[192]{0:T(256)S(1)}, f32[192]{0:T(256)S(1)}) all-reduce(f32[192]{0:T(256)S(1)} %exponential_reduce_fusion, f32[192]{0:T(256)S(1)} %get-tuple-element.3, f32[192]{0:T(256)S(1)} %get-tuple-element.2), channel_id=1, replica_groups=mesh['rows'=32,'vocab'=16] {'rows','vocab'}, use_global_device_ids=true, to_apply=%region_11.12 | all-reduce | flops 576 | bytes 4608 | tf_op jit(solution)/shard_map/psum | solution.py:46
  488.4 3.2 fusion.1
  491.6 0.0 all-reduce.3.cloned.1.call-update
  491.6 0.6 dynamic_slice.6
  492.2 480.6 %all-reduce.3.cloned.1.call-done = f32[192,5120]{1,0:T(8,128)} async-done(((f32[192,5120]{1,0:T(8,128)}), f32[192,5120]{1,0:T(8,128)}) %all-reduce.3.cloned.1.call-update) | async-done | bytes 3932176 | tf_op jit(solution)/shard_map/psum | solution.py:73
  972.9 1.4 dynamic_slice.7
  (4 shorter events, 0.0 us)
Async XLA Ops:
  7.2 177.1 %copy-start = (bf16[5120,280]{0,1:T(8,128)(2,1)S(1)}, bf16[5120,280]{0,1:T(8,128)(2,1)}, u32[]{:S(2)}) copy-start(bf16[5120,280]{0,1:T(8,128)(2,1)} %param.10) | copy-start | bytes 8601604
  7.2 101.3 %all-gather.8.cloned.1.call-start = ((), (), s32[]{:S(2)}) async-start(), calls=%async_computation.2 | async-start | bytes 2162688 | tf_op jit(solution)/shard_map/all_gather | solution.py:35
  29.2 150.9 %all-gather.6.cloned.1.call-start = ((), (), s32[]{:S(2)}) async-start(), calls=%async_computation.1 | async-start | bytes 2703360 | tf_op jit(solution)/shard_map/all_gather | solution.py:30
  47.2 925.7 %all-reduce.3.cloned.1.call-start = ((), (), s32[]{:S(2)}) async-start(), calls=%async_computation | async-start | bytes 7864320 | tf_op jit(solution)/shard_map/psum | solution.py:73
Sparse Core Ops, SparseCore 0:
  29.4 79.0 all-gather.7
  110.6 69.4 all-gather.5
  491.7 481.0 all-reduce.2
where the time goes:
time: 982 us; the launch traced here: 981 us
  waiting for transfers between devices  603 us (61%)
  blocking collectives  340 us (35%)
  between operations  13.8 us (1%)
  local copies, waits for them, and re-layouts  11.6 us (1%)
    psum x1, waiting for transfers between devices, on_device(): total_grad = lax.psum(partial_grad, ('rows', 'vocab'))  481 us
    pmax x2, blocking collectives, on_device(): lax.pmax((jnp.max(student_logits, axis=1), jnp.max(teacher_logits, axis=1...  201 us
    psum x1, blocking collectives, on_device(): lax.psum((jnp.sum(expo_s, axis=1), jnp.sum(expo_t, axis=1), jnp.sum(expo_...  100 us
    all_gather x1, waiting for transfers between devices, on_device(): lax.all_gather(student_feat, 'rows', axis=0, tiled=True)  63.6 us
    all_gather x1, waiting for transfers between devices, on_device(): lax.all_gather(teacher_feat, 'rows', axis=0, tiled=True)  58.3 us
    all_gather x1, blocking collectives, on_device(): lax.all_gather(teacher_hidden, 'vocab', axis=1, tiled=True)  22 us
  transfers between devices with their start and end apart: 3, of which 3 were waited for; matrix products, arithmetic and copies ran while one was open for 1% of the time, Pallas kernels for 0%

commit v1 on v0

v1 whole, which is shorter than its diff:
```python
import functools

import jax
import jax.numpy as jnp
from jax import lax
from jax.experimental import pallas as pl
from jax.experimental.pallas import tpu as pltpu
from jax.sharding import PartitionSpec as P

MESH = pl.DeviceIdType.MESH
F32 = jnp.float32
BF16 = jnp.bfloat16
LIVE = 112
HALF = 288

SIB_P, SIB_X, SIB_ST, SIB_R1, SIB_R5 = 0, 1, 17, 18, 22
ZF, ZN, ZST, ZR = 23, 26, 29, 44
PA, PB, PST, R2, R3 = 59, 62, 74, 89, 92
N_SEMS = 95


def iota(shape, dim):
    return lax.broadcasted_iota(jnp.int32, shape, dim)


def sixth(n):
    return lax.shift_right_logical(n * 171, 10)


def as_col(row, n):
    eye = iota((n, n), 0) == iota((n, n), 1)
    return jnp.sum(jnp.where(eye, row, 0.0), axis=1, keepdims=True)


def as_row(col, n):
    eye = iota((n, n), 0) == iota((n, n), 1)
    return jnp.sum(jnp.where(eye, col, 0.0), axis=0, keepdims=True)


def merge(stats):
    part = [stats[:, k, :] for k in range(5)]
    peak_s = jnp.max(part[0], axis=0, keepdims=True)
    peak_t = jnp.max(part[1], axis=0, keepdims=True)
    scale_s = jnp.exp(part[0] - peak_s)
    scale_t = jnp.exp(part[1] - peak_t)
    sum_s = jnp.sum(scale_s * part[2], axis=0, keepdims=True)
    sum_t = jnp.sum(scale_t * part[3], axis=0, keepdims=True)
    cross = jnp.sum(scale_s * part[4], axis=0, keepdims=True)
    return peak_s, peak_t, sum_s, sum_t, cross


def put_stats(ref, parts):
    row = iota((8, 128), 0)
    out = jnp.zeros((8, 128), F32)
    for k, part in enumerate(parts):
        out = jnp.where(row == k, part, out)
    ref[...] = out


def kernel(
    stop,
    sh_ref, th_ref, ws_hbm, wt_hbm, trow_ref, live_ref, branch_ref, ratio_ref,
    loss_ref, grad_ref,
    ws, wt, wide, parts, zbuf, sel, xbuf, logits, un1, un2, st_a, st_b, st_c,
    gt, sib_out, rb1, sb2, rb2, acc2, sb3, rb3, place, sb4, rb4, sb5, rb5, tail,
    head_sem, send, recv,
):
    r = lax.axis_index("rows")
    v = lax.axis_index("vocab")
    z = lax.div(r, 2)
    c = lax.rem(r, 2)
    x = lax.div(v, 4)
    y = lax.rem(v, 4)
    o = 1 - c
    a = x * o + y * c
    b = y * o + x * c

    def v_of(pa, pb):
        return (pa * 4 + pb) * o + (pb * 4 + pa) * c

    def v_sib(pa, pb):
        return (pa * 4 + pb) * c + (pb * 4 + pa) * o

    sibling = (z * 2 + o, v)

    def z_dev(d):
        return (lax.rem(z + d, 16) * 2 + c, v)

    def plane_dev(da, db):
        return (r, v_of(lax.rem(a + da, 4), lax.rem(b + db, 4)))

    def rcopy(src, dst, number, device):
        return pltpu.make_async_remote_copy(
            src_ref=src, dst_ref=dst, send_sem=send.at[number], recv_sem=recv.at[number],
            device_id=device, device_id_type=MESH,
        )

    pending = []

    def go(src, dst, number, device):
        copy = rcopy(src, dst, number, device)
        copy.start()
        pending.append(copy)

    def arrive(dst, number):
        rcopy(dst, dst, number, sibling).wait_recv()

    heads = [
        pltpu.make_async_copy(ws_hbm, ws, head_sem.at[0]),
        pltpu.make_async_copy(wt_hbm, wt, head_sem.at[1]),
    ]
    for copy in heads:
        copy.start()

    plane = [(da, db) for da in range(4) for db in range(4) if (da, db) != (0, 0)]
    barrier = pltpu.get_barrier_semaphore()
    pl.semaphore_signal(barrier, inc=1, device_id=sibling, device_id_type=MESH)
    for d in range(1, 16):
        pl.semaphore_signal(barrier, inc=1, device_id=z_dev(d), device_id_type=MESH)
    for da, db in plane:
        pl.semaphore_signal(barrier, inc=1, device_id=plane_dev(da, db), device_id_type=MESH)

    row16 = iota((16, 128), 0)
    wide[...] = jnp.zeros_like(wide)
    wide[0:6, 0:320] = sh_ref[...].astype(F32)
    sw = wide[...]
    s2 = sw[:, 256:384]
    s2_high = pltpu.roll(s2, 64, 1)
    th = th_ref[...].astype(F32)
    pack_s = jnp.zeros((16, 128), F32)
    pack_t = jnp.zeros((16, 128), F32)
    for i in range(6):
        pack_s = jnp.where(row16 == i, sw[i:i + 1, 0:128], pack_s)
        pack_s = jnp.where(row16 == 6 + i, sw[i:i + 1, 128:256], pack_s)
        pack_t = jnp.where(row16 == i, th[i:i + 1, 0:128], pack_t)
        pack_t = jnp.where(row16 == 6 + i, th[i:i + 1, 128:256], pack_t)
    for i in range(3):
        pack_s = jnp.where(row16 == 12 + i, s2[i:i + 1, :] + s2_high[i + 3:i + 4, :], pack_s)
    parts[0] = pack_s.astype(BF16)
    parts[1] = pack_t.astype(BF16)
    z_group = lax.rem(z, 4)
    z_slot = z_group * 4 + lax.div(z, 4)
    zbuf[z_slot, c] = parts[c]

    pl.semaphore_wait(barrier, 31)

    go(parts.at[o], zbuf.at[z_slot, c], SIB_P, sibling)

    live_row = live_ref[...].astype(F32)
    live_col = as_col(live_row, 32)
    owner_a, owner_b = iota((32, 32), 0), iota((32, 32), 1)
    before_col = jnp.sum(jnp.where(owner_b < owner_a, live_row, 0.0), axis=1, keepdims=True)
    before_row = jnp.sum(jnp.where(owner_a < owner_b, live_col, 0.0), axis=0, keepdims=True)
    pos = iota((1, 192), 1)
    pos_owner = sixth(pos)
    pos_slot = (pos - 6 * pos_owner).astype(F32)
    own = iota((32, 192), 0) == sixth(iota((32, 192), 1))
    rank = jnp.sum(jnp.where(own, before_col, 0.0), axis=0, keepdims=True) + pos_slot
    alive = jnp.sum(jnp.where(own, live_col, 0.0), axis=0, keepdims=True) > pos_slot
    rank = jnp.where(alive, rank, -1.0).astype(jnp.int32)
    pick = iota((128, 192), 0) == rank
    pos_of = jnp.sum(jnp.where(pick, pos.astype(F32), 0.0), axis=1, keepdims=True)
    teacher_of = jnp.sum(jnp.where(pick, trow_ref[...].astype(F32), 0.0), axis=1, keepdims=True)
    ratio_col = as_col(ratio_ref[...], 16)
    ratio_of = jnp.sum(
        jnp.where(iota((16, 192), 0) == branch_ref[...], ratio_col, 0.0), axis=0, keepdims=True
    )
    weight = as_row(jnp.sum(jnp.where(pick, ratio_of, 0.0), axis=1, keepdims=True), 128)
    source = jnp.where(c == 0, pos_of, teacher_of).astype(jnp.int32)[0:LIVE]
    src_owner = sixth(source)
    src_slot = source - 6 * src_owner
    src_z = lax.shift_right_logical(src_owner, 1)
    base = (
        (jnp.bitwise_and(src_z, 3) * 4 + lax.shift_right_logical(src_z, 2)) * 32
        + jnp.bitwise_and(src_owner, 1) * 16
    )
    low = src_slot < 3
    column = iota((LIVE, 512), 1)
    for k, at in enumerate((
        base + src_slot, base + 6 + src_slot, base + 12 + jnp.where(low, src_slot, src_slot - 3)
    )):
        sel[k] = jnp.where(column == at, 1.0, 0.0).astype(BF16)

    arrive(zbuf.at[z_slot, o], SIB_P)
    for n, d in enumerate((8, 4, 12)):
        go(zbuf.at[z_slot], zbuf.at[z_slot], ZF + n, z_dev(d))

    dest = iota((256, 1), 0)
    dest_z, q = lax.shift_right_logical(dest, 4), jnp.bitwise_and(dest, 15)

    def back(row, wanted):
        second = jnp.where(row >= 6, 1, 0)
        owner = 2 * dest_z + second
        slot = (row - 6 * second).astype(F32)
        mine = iota((256, 32), 1) == owner
        start = jnp.sum(jnp.where(mine, before_row, 0.0), axis=1, keepdims=True)
        count = jnp.sum(jnp.where(mine, live_row, 0.0), axis=1, keepdims=True)
        j = jnp.where(wanted & (slot < count), start + slot, -1.0).astype(jnp.int32)
        return jnp.where(iota((256, 128), 1) == j, 1.0, 0.0).astype(BF16)

    un1[...] = back(q, q < 12)
    for g in range(4):
        un2[g] = back((q - 12) * 4 + g, (q >= 12) & (q < 15))

    for n, d in enumerate((8, 4, 12)):
        arrive(zbuf.at[z_group * 4 + lax.rem(lax.div(z, 4) + 4 - d // 4, 4)], ZF + n)
    group = zbuf.at[pl.ds(z_group * 4, 4)]
    for n, d in enumerate((1, 15, 2)):
        go(group, group, ZN + n, z_dev(d))
    for n, d in enumerate((1, 15, 2)):
        arrive(zbuf.at[pl.ds(lax.rem(z_group + 16 - d, 4) * 4, 4)], ZN + n)

    if stop >= 2:
        raw = zbuf[...].reshape(512, 128)
        chunk = [jnp.dot(sel[k], raw, preferred_element_type=F32) for k in range(3)]
        turned = pltpu.roll(chunk[2], 64, 1)
        lane = iota((64, 128), 1)
        packed = jnp.where(
            lane < 64,
            jnp.where(low, chunk[2], turned)[0:64],
            jnp.where(low, turned, chunk[2])[48:112],
        )
        xbuf[c, v, 0:112] = chunk[0].astype(BF16)
        xbuf[c, v, 112:224] = chunk[1].astype(BF16)
        xbuf[c, v, 224:288] = packed.astype(BF16)

        def spread(pa, n):
            block = xbuf.at[c, v_of(pa, b)]
            for k, d in enumerate((2, 1, 3)):
                go(block, block, PB + 3 * n + k, plane_dev(0, d))
            go(block, block, SIB_X + n, sibling)

        mine = xbuf.at[c, v]
        for k, d in enumerate((1, 3, 2)):
            go(mine, mine, PA + k, plane_dev(d, 0))
        spread(a, 0)
        for k, d in enumerate((1, 3, 2)):
            pa = lax.rem(a + 4 - d, 4)
            arrive(xbuf.at[c, v_of(pa, b)], PA + k)
            spread(pa, k + 1)
        for n, d0 in enumerate((0, 1, 3, 2)):
            for k, d in enumerate((2, 1, 3)):
                block = xbuf.at[c, v_of(lax.rem(a + 4 - d0, 4), lax.rem(b + 4 - d, 4))]
                arrive(block, PB + 3 * n + k)
                go(block, block, SIB_X + 4 + 3 * n + k, sibling)
        for n, d0 in enumerate((0, 1, 3, 2)):
            pa = lax.rem(b + 4 - d0, 4)
            arrive(xbuf.at[o, v_sib(pa, a)], SIB_X + n)
        for n, d0 in enumerate((0, 1, 3, 2)):
            for k, d in enumerate((2, 1, 3)):
                pa, pb = lax.rem(b + 4 - d0, 4), lax.rem(a + 4 - d, 4)
                arrive(xbuf.at[o, v_sib(pa, pb)], SIB_X + 4 + 3 * n + k)
    for copy in heads:
        copy.wait()

    if stop >= 3:
        lane = iota((LIVE, 128), 1)
        keep = (lane < 64) == (iota((LIVE, 128), 0) < 64)
        acc_s = jnp.zeros((LIVE, 280), F32)
        acc_t = jnp.zeros((LIVE, 280), F32)
        for pair in range(8):
            left, right = [], []
            for w in (2 * pair, 2 * pair + 1):
                block = jnp.concatenate([xbuf[0, w, 0:112], xbuf[0, w, 112:224]], axis=1)
                acc_s += jnp.dot(block, ws[w * 320:w * 320 + 256], preferred_element_type=F32)
                block = jnp.concatenate([xbuf[1, w, 0:112], xbuf[1, w, 112:224]], axis=1)
                acc_t += jnp.dot(block, wt[w * 256:w * 256 + 256], preferred_element_type=F32)
                rest = jnp.concatenate([xbuf[0, w, 224:288], xbuf[0, w, 240:288]], axis=0)
                left.append(jnp.where(keep, rest, jnp.zeros_like(rest)))
                right += [ws[w * 320 + 256:w * 320 + 320]] * 2
            acc_s += jnp.dot(
                jnp.concatenate(left, axis=1), jnp.concatenate(right, axis=0),
                preferred_element_type=F32,
            )
        logits[...] = jnp.zeros_like(logits)
        logits[0, 0:LIVE, 0:280] = acc_s
        logits[1, 0:LIVE, 0:280] = acc_t
        student = jnp.transpose(logits[0])[0:280]
        teacher = jnp.transpose(logits[1])[0:280]
        diff = student - teacher
        peak_s = jnp.max(student, axis=0, keepdims=True)
        peak_t = jnp.max(teacher, axis=0, keepdims=True)
        expo = jnp.exp(student - peak_s)
        put_stats(st_a.at[c], (
            peak_s, peak_t,
            jnp.sum(expo, axis=0, keepdims=True),
            jnp.sum(jnp.exp(teacher - peak_t), axis=0, keepdims=True),
            jnp.sum(expo * diff, axis=0, keepdims=True),
        ))

    if stop >= 4:
        go(st_a.at[c], st_a.at[c], SIB_ST, sibling)
        arrive(st_a.at[o], SIB_ST)
        put_stats(st_b.at[v], merge(st_a[...]))
        for n, (da, db) in enumerate(plane):
            go(st_b.at[v], st_b.at[v], PST + n, plane_dev(da, db))
        for n, (da, db) in enumerate(plane):
            arrive(st_b.at[v_of(lax.rem(a + 4 - da, 4), lax.rem(b + 4 - db, 4))], PST + n)
        put_stats(st_c.at[z], merge(st_b[...]))
        for n, d in enumerate(range(1, 16)):
            go(st_c.at[z], st_c.at[z], ZST + n, z_dev(d))
        for n, d in enumerate(range(1, 16)):
            arrive(st_c.at[lax.rem(z + 16 - d, 16)], ZST + n)
        peak_s, peak_t, sum_s, sum_t, cross = merge(st_c[...])
        lse_s = peak_s + jnp.log(sum_s)
        lse_t = peak_t + jnp.log(sum_t)
        divergence = cross / sum_s - lse_s + lse_t
        loss = as_col(weight * divergence, 128)
        ours = iota((1, 32), 1) == r
        start = jnp.sum(jnp.where(ours, before_row, 0.0), axis=1, keepdims=True)
        count = jnp.sum(jnp.where(ours, live_row, 0.0), axis=1, keepdims=True)
        slot = iota((1, 128), 1).astype(F32)
        at = jnp.where(slot < count, start + slot, -1.0).astype(jnp.int32)
        loss_ref[...] = jnp.sum(
            jnp.where(iota((128, 128), 0) == at, loss, 0.0), axis=0, keepdims=True
        )
        gt[...] = (
            weight * jnp.exp(student - lse_s) * (diff - lse_s + lse_t - divergence)
        ).astype(BF16)

    if stop >= 5:
        order = (2, 1, 3, 0)
        g = gt[...]

        def back_product(w, half):
            at = pl.multiple_of(w * 320 + half * 160, 32)
            return jnp.dot(ws[pl.ds(at, 160), :], g, preferred_element_type=F32)

        for d in order:
            pb = lax.rem(a + d, 4)
            for pa in range(4):
                sib_out[d, pa] = back_product(v_sib(pa, pb), o).astype(BF16)
            go(sib_out.at[d], rb1.at[d], SIB_R1 + d, sibling)
        for d in order:
            pb = lax.rem(b + d, 4)
            arrive(rb1.at[d], SIB_R1 + d)
            for pa in range(4):
                total = back_product(v_of(pa, pb), c) + rb1[d, pa].astype(F32)
                if d:
                    sb2[d - 1, pa] = total.astype(BF16)
                else:
                    acc2[pa] = total
            if d:
                go(sb2.at[d - 1], rb2.at[d - 1], R2 + d - 1, plane_dev(0, d))
        for d in (1, 3, 2):
            arrive(rb2.at[d - 1], R2 + d - 1)
        for d in (2, 1, 3, 0):
            pa = lax.rem(a + d, 4)
            total = acc2[pa]
            for k in range(3):
                total += rb2[k, pa].astype(F32)
            if d:
                sb3[d - 1] = total.astype(BF16)
                go(sb3.at[d - 1], rb3.at[d - 1], R3 + d - 1, plane_dev(d, 0))
        for d in (1, 3, 2):
            arrive(rb3.at[d - 1], R3 + d - 1)
            total += rb3[d - 1].astype(F32)
        total = total.astype(BF16)

    if stop >= 6:
        place[...] = jnp.zeros_like(place)
        for k in range(4):
            place[k, 32 * k:32 * k + 32] = total[128:160]
        nt = (((1,), (1,)), ((), ()))
        spread_out = lax.dot_general(un1[...], total[0:128], nt, preferred_element_type=F32)
        for k in range(4):
            spread_out += lax.dot_general(un2[k], place[k], nt, preferred_element_type=F32)
        sb4[...] = spread_out.astype(BF16).reshape(16, 16, 128)
        rb4[z] = sb4[z]
        for n, d in enumerate(range(1, 16)):
            go(sb4.at[lax.rem(z + d, 16)], rb4.at[z], ZR + n, z_dev(d))
        for n, d in enumerate(range(1, 16)):
            arrive(rb4.at[lax.rem(z + 16 - d, 16)], ZR + n)
        full = jnp.sum(rb4[...].astype(F32), axis=0)
        sb5[c] = full
        go(sb5.at[c], sb5.at[c], SIB_R5, sibling)
        arrive(sb5.at[o], SIB_R5)
        grads = []
        for h in range(2):
            block = sb5[h]
            for row in range(12):
                at = 32 * (row % 4)
                tail[h, row:row + 1, 0:32] = block[12 + row // 4:13 + row // 4, at:at + 32]
            grads.append(jnp.where(c == 0, block[0:6], block[6:12]))
            grads.append(jnp.where(c == 0, tail[h, 0:6], tail[h, 6:12])[:, 0:32])
        grad_ref[:, 0:128] = grads[0]
        grad_ref[:, 128:160] = grads[1]
        grad_ref[:, 160:288] = grads[2]
        grad_ref[:, 288:320] = grads[3]
    else:
        grad_ref[...] = jnp.zeros_like(grad_ref)
        if stop < 4:
            loss_ref[...] = jnp.zeros_like(loss_ref)

    for copy in pending:
        copy.wait_send()


def on_device(
    student_hidden, teacher_hidden, student_head, teacher_head,
    teacher_row, live_counts, branch_id, branch_ratio, stop=99,
):
    vmem = pl.BlockSpec(memory_space=pltpu.VMEM)
    hbm = pl.BlockSpec(memory_space=pl.ANY)
    loss, grad = pl.pallas_call(
        functools.partial(kernel, stop),
        out_shape=(
            jax.ShapeDtypeStruct((1, 128), F32),
            jax.ShapeDtypeStruct((6, 320), F32),
        ),
        in_specs=[vmem, vmem, hbm, hbm, vmem, vmem, vmem, vmem],
        out_specs=(vmem, vmem),
        scratch_shapes=[
            pltpu.VMEM((5120, 280), BF16),
            pltpu.VMEM((4096, 280), BF16),
            pltpu.VMEM((8, 384), F32),
            pltpu.VMEM((2, 16, 128), BF16),
            pltpu.VMEM((16, 2, 16, 128), BF16),
            pltpu.VMEM((3, LIVE, 512), BF16),
            pltpu.VMEM((2, 16, HALF, 128), BF16),
            pltpu.VMEM((2, 128, 384), F32),
            pltpu.VMEM((256, 128), BF16),
            pltpu.VMEM((4, 256, 128), BF16),
            pltpu.VMEM((2, 8, 128), F32),
            pltpu.VMEM((16, 8, 128), F32),
            pltpu.VMEM((16, 8, 128), F32),
            pltpu.VMEM((280, 128), BF16),
            pltpu.VMEM((4, 4, 160, 128), BF16),
            pltpu.VMEM((4, 4, 160, 128), BF16),
            pltpu.VMEM((3, 4, 160, 128), BF16),
            pltpu.VMEM((3, 4, 160, 128), BF16),
            pltpu.VMEM((4, 160, 128), F32),
            pltpu.VMEM((3, 160, 128), BF16),
            pltpu.VMEM((3, 160, 128), BF16),
            pltpu.VMEM((4, 128, 128), BF16),
            pltpu.VMEM((16, 16, 128), BF16),
            pltpu.VMEM((16, 16, 128), BF16),
            pltpu.VMEM((2, 16, 128), F32),
            pltpu.VMEM((8, 128), F32),
            pltpu.VMEM((2, 16, 128), F32),
            pltpu.SemaphoreType.DMA((2,)),
            pltpu.SemaphoreType.DMA((N_SEMS,)),
            pltpu.SemaphoreType.DMA((N_SEMS,)),
        ],
        compiler_params=pltpu.CompilerParams(
            collective_id=0, has_side_effects=True, vmem_limit_bytes=48 * 1024 * 1024
        ),
    )(
        student_hidden, teacher_hidden, student_head, teacher_head,
        teacher_row.reshape(1, -1), live_counts.reshape(1, -1),
        branch_id.reshape(1, -1), branch_ratio.reshape(1, -1),
    )
    return loss[0, 0:6], grad


def solution(mesh, stop=99):
    in_specs = (
        P("rows", "vocab"),
        P("rows", "vocab"),
        P(None, ("rows", "vocab")),
        P(None, ("rows", "vocab")),
        P(),
        P(),
        P(),
        P(),
    )
    out_specs = (P("rows"), P("rows", "vocab"))
    return jax.shard_map(
        functools.partial(on_device, stop=stop), mesh=mesh, in_specs=in_specs,
        out_specs=out_specs, check_vma=False,
    )
```

time: 982 us -> 94.4 us (0.10)
  waiting for transfers between devices: 603 us -> 0 us
  blocking collectives: 340 us -> 0 us
  Pallas kernels: 0 us -> 83.3 us
  between operations: 13.8 us -> 0.72 us
    psum x1 -> x0, waiting for transfers between devices: 481 us -> none  [on_device(): total_grad = lax.psum(partial_grad, ('rows', 'vocab'))]
    pmax x2 -> x0, blocking collectives: 201 us -> none  [on_device(): lax.pmax((jnp.max(student_logits, axis=1), jnp.max(teacher_logits, axis=1...]
    all_gather x2 -> x0, waiting for transfers between devices: 122 us -> none  [the longest x1 63.6 us: on_device(): lax.all_gather(student_feat, 'rows', axis=0, tiled=True)]
    psum x1 -> x0, blocking collectives: 100 us -> none  [on_device(): lax.psum((jnp.sum(expo_s, axis=1), jnp.sum(expo_t, axis=1), jnp.sum(expo_...]
    pallas_call x0 -> x1, Pallas kernels: none -> 83.3 us  [on_device(): pl.pallas_call(functools.partial(kernel, stop), out_shape=(jax.ShapeDtype...]
    all_gather x2 -> x0, blocking collectives: 39.1 us -> none  [the longest x1 22 us: on_device(): lax.all_gather(teacher_hidden, 'vocab', axis=1, tiled=True)]
  transfers between devices with their start and end apart: 3 -> 0, of which waited for: 3 -> 0; matrix products, arithmetic and copies ran while one was open for 1% -> 0% of each run, Pallas kernels for 0% -> 0%
where the time goes in v1:
time: 94.4 us; the launch traced here: 94.1 us
  Pallas kernels  83.3 us (88%)
  local copies, waits for them, and re-layouts  10.1 us (11%)
    pallas_call x1, Pallas kernels, on_device(): pl.pallas_call(functools.partial(kernel, stop), out_shape=(jax.ShapeDtype...  83.3 us
    unnamed x15, local copies, waits for them, and re-layouts  9.54 us

profile of v1, /device:TPU:1, one launch (start us, length us, event | category | flops | bytes accessed | tf_op | source)
XLA Modules:
  0.0 94.1 jit_solution(2940297347988515438)
XLA Ops:
  0.6 3.3 %copy.11.wt_hbm = bf16[4096,280]{1,0:T(8,128)(2,1)S(1)} copy(bf16[4096,280]{0,1:T(8,128)(2,1)} %param.11) | data formatting | bytes 4587520 | tf_op args[3]
  3.9 0.0 copy-start
  3.9 0.0 copy-start.1
  3.9 0.0 copy-start.2
  3.9 0.0 copy-start.3
  3.9 0.0 copy-start.4
  4.0 0.0 copy-start.5
  4.0 5.6 %copy.10.ws_hbm = bf16[5120,280]{1,0:T(8,128)(2,1)} copy(bf16[5120,280]{0,1:T(8,128)(2,1)} %param.10) | data formatting | bytes 5734400 | tf_op args[2]
  9.6 0.0 copy-done
  9.6 0.0 copy-done.1
  9.6 0.0 copy-done.2
  9.6 0.0 copy-done.3
  9.6 0.0 copy-done.4
  9.6 0.0 copy-done.5
  9.7 83.3 %shard_map.95 = (f32[1,128]{1,0:T(1,128)S(1)}, f32[6,320]{1,0:T(8,128)S(1)}) custom-call(bf16[6,320]{1,0:T(8,128)(2,1)S(1)} %copy-done, bf16[6,256]{1,0:T(8,128)(2,1)S(1)} %copy-done.1, bf16[5120,280]{1,0:T(8,128)(2,1)} %copy.10.ws_hbm, bf16[4096,280]{1,0:T(8,128)(2,1)S(1)} %copy.11.wt_hbm, s32[1,192]{1,0:T(1,128)S(1)} %bitcast.6, s32[1,32]{1,0:T(1,128)S(1)} %bitcast.8, ...), custom_call_target="tpu_custom_call" | custom-call | tf_op jit(solution)/shard_map/pallas_call | solution.py:405
  93.0 0.5 slice_bitcast_fusion
  93.5 0.6 copy.13
Async XLA Ops:
  3.9 5.7 %copy-start = (bf16[6,320]{1,0:T(8,128)(2,1)S(1)}, bf16[6,320]{1,0:T(8,128)(2,1)}, u32[]{:S(2)}) copy-start(bf16[6,320]{1,0:T(8,128)(2,1)} %sh_ref.1) | copy-start | bytes 11524
  3.9 5.7 %copy-start.1 = (bf16[6,256]{1,0:T(8,128)(2,1)S(1)}, bf16[6,256]{1,0:T(8,128)(2,1)}, u32[]{:S(2)}) copy-start(bf16[6,256]{1,0:T(8,128)(2,1)} %th_ref.1) | copy-start | bytes 9220
  3.9 5.7 %copy-start.2 = (s32[192]{0:T(256)S(1)}, s32[192]{0:T(256)}, u32[]{:S(2)}) copy-start(s32[192]{0:T(256)} %param.12) | copy-start | bytes 2308
  3.9 5.7 %copy-start.3 = (s32[192]{0:T(256)S(1)}, s32[192]{0:T(256)}, u32[]{:S(2)}) copy-start(s32[192]{0:T(256)} %param.14) | copy-start | bytes 2308
  3.9 5.7 %copy-start.4 = (s32[32]{0:T(128)S(1)}, s32[32]{0:T(128)}, u32[]{:S(2)}) copy-start(s32[32]{0:T(128)} %param.13) | copy-start | bytes 388
  4.0 5.7 %copy-start.5 = (f32[16]{0:T(128)S(1)}, f32[16]{0:T(128)}, u32[]{:S(2)}) copy-start(f32[16]{0:T(128)} %param.15) | copy-start | bytes 196

commit v2 on v1

v2 whole, which is shorter than its diff:
```python
import jax
import jax.numpy as jnp
from jax import lax
from jax.experimental import pallas as pl
from jax.experimental.pallas import tpu as pltpu
from jax.sharding import PartitionSpec as P

MESH = pl.DeviceIdType.MESH
F32 = jnp.float32
BF16 = jnp.bfloat16
LIVE = 112
HALF = 288

SIB_P, SIB_X, SIB_ST, SIB_W, SIB_G, SIB_R5 = 0, 1, 17, 18, 20, 21
ZP, ZST, ZR = 22, 37, 52
PA, PB, PST, R2, R3 = 67, 70, 82, 97, 100
N_SEMS = 103
Z_ORDER = (8, 7, 9, 6, 10, 5, 11, 4, 12, 3, 13, 2, 14, 1, 15)


def iota(shape, dim):
    return lax.broadcasted_iota(jnp.int32, shape, dim)


def sixth(n):
    return lax.shift_right_logical(n * 171, 10)


def as_col(row, n):
    eye = iota((n, n), 0) == iota((n, n), 1)
    return jnp.sum(jnp.where(eye, row, 0.0), axis=1, keepdims=True)


def as_row(col, n):
    eye = iota((n, n), 0) == iota((n, n), 1)
    return jnp.sum(jnp.where(eye, col, 0.0), axis=0, keepdims=True)


def merge(stats):
    part = [stats[:, k, :] for k in range(5)]
    peak_s = jnp.max(part[0], axis=0, keepdims=True)
    peak_t = jnp.max(part[1], axis=0, keepdims=True)
    scale_s = jnp.exp(part[0] - peak_s)
    scale_t = jnp.exp(part[1] - peak_t)
    sum_s = jnp.sum(scale_s * part[2], axis=0, keepdims=True)
    sum_t = jnp.sum(scale_t * part[3], axis=0, keepdims=True)
    cross = jnp.sum(scale_s * part[4], axis=0, keepdims=True)
    return peak_s, peak_t, sum_s, sum_t, cross


def put_stats(ref, parts):
    row = iota((8, 128), 0)
    out = jnp.zeros((8, 128), F32)
    for k, part in enumerate(parts):
        out = jnp.where(row == k, part, out)
    ref[...] = out


def kernel(
    sh_hbm, th_hbm, ws_hbm, wt_hbm, trow_hbm, live_hbm, branch_hbm, ratio_hbm,
    loss_ref, grad_ref,
    sh_ref, th_ref, trow_ref, live_ref, branch_ref, ratio_ref,
    wst, wtt, wh, wsib, wide, parts, zbuf, sel, xbuf, un1, un2, st_a, st_b, st_c,
    g2, sb2, rb2, acc2, sb3, rb3, place, sb4, rb4, sb5, tail,
    head_sem, small_sem, send, recv,
):
    r = lax.axis_index("rows")
    v = lax.axis_index("vocab")
    z = lax.div(r, 2)
    c = lax.rem(r, 2)
    x = lax.div(v, 4)
    y = lax.rem(v, 4)
    o = 1 - c
    a = x * o + y * c
    b = y * o + x * c

    def v_of(pa, pb):
        return (pa * 4 + pb) * o + (pb * 4 + pa) * c

    def v_sib(pa, pb):
        return (pa * 4 + pb) * c + (pb * 4 + pa) * o

    sibling = (z * 2 + o, v)

    def z_dev(d):
        return (lax.rem(z + d, 16) * 2 + c, v)

    def plane_dev(da, db):
        return (r, v_of(lax.rem(a + da, 4), lax.rem(b + db, 4)))

    def rcopy(src, dst, number, device):
        return pltpu.make_async_remote_copy(
            src_ref=src, dst_ref=dst, send_sem=send.at[number], recv_sem=recv.at[number],
            device_id=device, device_id_type=MESH,
        )

    pending = []

    def go(src, dst, number, device):
        copy = rcopy(src, dst, number, device)
        copy.start()
        pending.append(copy)

    def arrive(dst, number):
        rcopy(dst, dst, number, sibling).wait_recv()

    heads = [
        pltpu.make_async_copy(ws_hbm, wst, head_sem.at[0]),
        pltpu.make_async_copy(wt_hbm, wtt, head_sem.at[1]),
    ]
    small = [
        pltpu.make_async_copy(src, dst, small_sem.at[n])
        for n, (src, dst) in enumerate((
            (sh_hbm, sh_ref), (th_hbm, th_ref), (trow_hbm, trow_ref),
            (live_hbm, live_ref), (branch_hbm, branch_ref), (ratio_hbm, ratio_ref),
        ))
    ]
    for copy in small + heads:
        copy.start()

    plane = [(da, db) for da in range(4) for db in range(4) if (da, db) != (0, 0)]
    plane.sort(key=lambda at: -min(at[0], 4 - at[0]) - min(at[1], 4 - at[1]))
    barrier = pltpu.get_barrier_semaphore()
    for d in Z_ORDER:
        pl.semaphore_signal(barrier, inc=1, device_id=z_dev(d), device_id_type=MESH)
    for da, db in plane:
        pl.semaphore_signal(barrier, inc=1, device_id=plane_dev(da, db), device_id_type=MESH)
    pl.semaphore_signal(barrier, inc=1, device_id=sibling, device_id_type=MESH)
    for copy in small:
        copy.wait()

    row16 = iota((16, 128), 0)
    wide[...] = jnp.zeros_like(wide)
    wide[0:6, 0:320] = sh_ref[...].astype(F32)
    sw = wide[...]
    odd = lax.rem(v, 2) == 1
    sw_odd = jnp.concatenate([pltpu.roll(sw, 320, 1)[:, 0:256], sw[:, 0:128]], axis=1)
    sw = jnp.where(odd, sw_odd, sw)
    s2 = jnp.where(iota((8, 128), 1) < 64, sw[:, 256:384], 0.0)
    s2_high = pltpu.roll(s2, 64, 1)
    th = th_ref[...].astype(F32)
    pack_s = jnp.zeros((16, 128), F32)
    pack_t = jnp.zeros((16, 128), F32)
    for i in range(6):
        pack_s = jnp.where(row16 == i, sw[i:i + 1, 0:128], pack_s)
        pack_s = jnp.where(row16 == 6 + i, sw[i:i + 1, 128:256], pack_s)
        pack_t = jnp.where(row16 == i, th[i:i + 1, 0:128], pack_t)
        pack_t = jnp.where(row16 == 6 + i, th[i:i + 1, 128:256], pack_t)
    for i in range(3):
        pack_s = jnp.where(row16 == 12 + i, s2[i:i + 1, :] + s2_high[i + 3:i + 4, :], pack_s)
    parts[0] = pack_s.astype(BF16)
    parts[1] = pack_t.astype(BF16)
    zbuf[z, c] = parts[c]

    live_row = live_ref[...].astype(F32)
    live_col = as_col(live_row, 32)
    owner_a, owner_b = iota((32, 32), 0), iota((32, 32), 1)
    before_col = jnp.sum(jnp.where(owner_b < owner_a, live_row, 0.0), axis=1, keepdims=True)
    before_row = jnp.sum(jnp.where(owner_a < owner_b, live_col, 0.0), axis=0, keepdims=True)
    pos = iota((1, 192), 1)
    pos_owner = sixth(pos)
    pos_slot = (pos - 6 * pos_owner).astype(F32)
    own = iota((32, 192), 0) == sixth(iota((32, 192), 1))
    rank = jnp.sum(jnp.where(own, before_col, 0.0), axis=0, keepdims=True) + pos_slot
    alive = jnp.sum(jnp.where(own, live_col, 0.0), axis=0, keepdims=True) > pos_slot
    rank = jnp.where(alive, rank, -1.0).astype(jnp.int32)
    pick = iota((128, 192), 0) == rank
    pos_of = jnp.sum(jnp.where(pick, pos.astype(F32), 0.0), axis=1, keepdims=True)
    teacher_of = jnp.sum(jnp.where(pick, trow_ref[...].astype(F32), 0.0), axis=1, keepdims=True)
    ratio_col = as_col(ratio_ref[...], 16)
    ratio_of = jnp.sum(
        jnp.where(iota((16, 192), 0) == branch_ref[...], ratio_col, 0.0), axis=0, keepdims=True
    )
    weight = as_row(jnp.sum(jnp.where(pick, ratio_of, 0.0), axis=1, keepdims=True), 128)
    source = jnp.where(c == 0, pos_of, teacher_of).astype(jnp.int32)[0:LIVE]
    src_owner = sixth(source)
    src_slot = source - 6 * src_owner
    src_z = lax.shift_right_logical(src_owner, 1)
    base = src_z * 32 + jnp.bitwise_and(src_owner, 1) * 16
    low = src_slot < 3
    column = iota((LIVE, 512), 1)
    for k, at in enumerate((
        base + src_slot, base + 6 + src_slot, base + 12 + jnp.where(low, src_slot, src_slot - 3)
    )):
        sel[k] = jnp.where(column == at, 1.0, 0.0).astype(BF16)

    dest = iota((256, 1), 0)
    dest_z, q = lax.shift_right_logical(dest, 4), jnp.bitwise_and(dest, 15)

    def back(row, wanted):
        second = jnp.where(row >= 6, 1, 0)
        owner = 2 * dest_z + second
        slot = (row - 6 * second).astype(F32)
        mine = iota((256, 32), 1) == owner
        start = jnp.sum(jnp.where(mine, before_row, 0.0), axis=1, keepdims=True)
        count = jnp.sum(jnp.where(mine, live_row, 0.0), axis=1, keepdims=True)
        j = jnp.where(wanted & (slot < count), start + slot, -1.0).astype(jnp.int32)
        return jnp.where(iota((256, 128), 1) == j, 1.0, 0.0).astype(BF16)

    un1[...] = back(q, q < 12)
    for g in range(4):
        un2[g] = back((q - 12) * 4 + g, (q >= 12) & (q < 15))

    pl.semaphore_wait(barrier, 31)
    go(parts.at[o], zbuf.at[z, c], SIB_P, sibling)
    arrive(zbuf.at[z, o], SIB_P)
    for n, d in enumerate(Z_ORDER):
        go(zbuf.at[z], zbuf.at[z], ZP + n, z_dev(d))

    heads[0].wait()
    for part in range(2):
        for u in range(4 * part, 4 * part + 4):
            turned = jnp.transpose(wst[:, 640 * u:640 * u + 640])
            for k in range(4):
                wh[k % 2, 2 * u + k // 2] = turned[160 * k:160 * k + 160]
        where = pl.ds(8 * part, 8)
        go(wh.at[o, where], wsib.at[where], SIB_W + part, sibling)
    for n, d in enumerate(Z_ORDER):
        arrive(zbuf.at[lax.rem(z + 16 - d, 16)], ZP + n)
    for part in range(2):
        where = pl.ds(8 * part, 8)
        arrive(wsib.at[where], SIB_W + part)
    raw = zbuf[...].reshape(512, 128)
    chunk = [jnp.dot(sel[k], raw, preferred_element_type=F32) for k in range(3)]
    turned = pltpu.roll(chunk[2], 64, 1)
    lane = iota((64, 128), 1)
    in_low, in_high = jnp.where(low, chunk[2], turned), jnp.where(low, turned, chunk[2])
    packed = jnp.where(
        odd,
        jnp.where(lane < 64, in_low[48:112], in_high[0:64]),
        jnp.where(lane < 64, in_low[0:64], in_high[48:112]),
    )
    xbuf[c, v, 0:112] = chunk[0].astype(BF16)
    xbuf[c, v, 112:224] = chunk[1].astype(BF16)
    xbuf[c, v, 224:288] = packed.astype(BF16)

    def spread(pa, n):
        block = xbuf.at[c, v_of(pa, b)]
        for k, d in enumerate((2, 1, 3)):
            go(block, block, PB + 3 * n + k, plane_dev(0, d))
        go(block, block, SIB_X + n, sibling)

    mine = xbuf.at[c, v]
    for k, d in enumerate((1, 3, 2)):
        go(mine, mine, PA + k, plane_dev(d, 0))
    spread(a, 0)
    for k, d in enumerate((1, 3, 2)):
        pa = lax.rem(a + 4 - d, 4)
        arrive(xbuf.at[c, v_of(pa, b)], PA + k)
        spread(pa, k + 1)
    for n, d0 in enumerate((0, 1, 3, 2)):
        for k, d in enumerate((2, 1, 3)):
            block = xbuf.at[c, v_of(lax.rem(a + 4 - d0, 4), lax.rem(b + 4 - d, 4))]
            arrive(block, PB + 3 * n + k)
            go(block, block, SIB_X + 4 + 3 * n + k, sibling)
    for n, d0 in enumerate((0, 1, 3, 2)):
        pa = lax.rem(b + 4 - d0, 4)
        arrive(xbuf.at[o, v_sib(pa, a)], SIB_X + n)
    for n, d0 in enumerate((0, 1, 3, 2)):
        for k, d in enumerate((2, 1, 3)):
            pa, pb = lax.rem(b + 4 - d0, 4), lax.rem(a + 4 - d, 4)
            arrive(xbuf.at[o, v_sib(pa, pb)], SIB_X + 4 + 3 * n + k)
    heads[1].wait()

    nt = (((1,), (1,)), ((), ()))
    lane = iota((64, 128), 1)
    student = jnp.zeros((280, LIVE), F32)
    teacher = jnp.zeros((280, LIVE), F32)
    for u in range(8):
        even, odd_ = 2 * u, 2 * u + 1
        first, second = xbuf[0, even, 224:288].astype(F32), xbuf[0, odd_, 224:288].astype(F32)
        top = jnp.where(lane < 64, first, second)
        rest = pltpu.roll(jnp.where(lane < 64, second, first), 64, 1)[16:64]
        block = jnp.concatenate(
            [
                xbuf[0, even, 0:112], xbuf[0, even, 112:224],
                jnp.concatenate([top, rest], axis=0).astype(BF16),
                xbuf[0, odd_, 0:112], xbuf[0, odd_, 112:224],
            ],
            axis=1,
        )
        student += lax.dot_general(
            wst[:, 640 * u:640 * u + 640], block, nt, preferred_element_type=F32
        )
        block = jnp.concatenate(
            [
                xbuf[1, even, 0:112], xbuf[1, even, 112:224],
                xbuf[1, odd_, 0:112], xbuf[1, odd_, 112:224],
            ],
            axis=1,
        )
        teacher += lax.dot_general(
            wtt[:, 512 * u:512 * u + 512], block, nt, preferred_element_type=F32
        )
    zeros = jnp.zeros((280, 128 - LIVE), F32)
    student = jnp.concatenate([student, zeros], axis=1)
    teacher = jnp.concatenate([teacher, zeros], axis=1)
    diff = student - teacher
    peak_s = jnp.max(student, axis=0, keepdims=True)
    peak_t = jnp.max(teacher, axis=0, keepdims=True)
    expo = jnp.exp(student - peak_s)
    put_stats(st_a.at[c], (
        peak_s, peak_t,
        jnp.sum(expo, axis=0, keepdims=True),
        jnp.sum(jnp.exp(teacher - peak_t), axis=0, keepdims=True),
        jnp.sum(expo * diff, axis=0, keepdims=True),
    ))

    go(st_a.at[c], st_a.at[c], SIB_ST, sibling)
    arrive(st_a.at[o], SIB_ST)
    chip = merge(st_a[...])
    put_stats(st_b.at[v], chip)
    for n, (da, db) in enumerate(plane):
        go(st_b.at[v], st_b.at[v], PST + n, plane_dev(da, db))

    mass = expo * jnp.exp(peak_s - chip[0])
    g2[c, 0:280, 0:128] = (mass * (diff - chip[4] / chip[2])).astype(BF16)
    g2[c, 0:280, 128:256] = mass.astype(BF16)
    go(g2.at[c], g2.at[c], SIB_G, sibling)
    arrive(g2.at[o], SIB_G)

    def products(d):
        pb = lax.rem(b + d, 4)
        for pa in range(4):
            w = v_of(pa, pb)
            total = jnp.dot(wh[c, w], g2[c, 0:280], preferred_element_type=F32)
            total += jnp.dot(wsib[w], g2[o, 0:280], preferred_element_type=F32)
            if d:
                sb2[d - 1, pa] = total.astype(BF16)
            else:
                acc2[pa] = total

    for d in (2, 1, 3):
        products(d)
        go(sb2.at[d - 1], rb2.at[d - 1], R2 + d - 1, plane_dev(0, d))
    for n, (da, db) in enumerate(plane):
        arrive(st_b.at[v_of(lax.rem(a + 4 - da, 4), lax.rem(b + 4 - db, 4))], PST + n)
    put_stats(st_c.at[z], merge(st_b[...]))
    for n, d in enumerate(Z_ORDER):
        go(st_c.at[z], st_c.at[z], ZST + n, z_dev(d))
    products(0)
    for d in (1, 3, 2):
        arrive(rb2.at[d - 1], R2 + d - 1)
    for n, d in enumerate(Z_ORDER):
        arrive(st_c.at[lax.rem(z + 16 - d, 16)], ZST + n)
    peak_s, peak_t, sum_s, sum_t, cross = merge(st_c[...])
    lse_s = peak_s + jnp.log(sum_s)
    lse_t = peak_t + jnp.log(sum_t)
    divergence = cross / sum_s - lse_s + lse_t
    loss = as_col(weight * divergence, 128)
    ours = iota((1, 32), 1) == r
    start = jnp.sum(jnp.where(ours, before_row, 0.0), axis=1, keepdims=True)
    count = jnp.sum(jnp.where(ours, live_row, 0.0), axis=1, keepdims=True)
    slot = iota((1, 128), 1).astype(F32)
    at = jnp.where(slot < count, start + slot, -1.0).astype(jnp.int32)
    loss_ref[...] = jnp.sum(
        jnp.where(iota((128, 128), 0) == at, loss, 0.0), axis=0, keepdims=True
    )
    mean = cross / sum_s
    scales, shifts = [], []
    for d in range(4):
        shard = st_b[v_of(a, lax.rem(b + 4 - d, 4))]
        scales.append(weight * jnp.exp(shard[0:1] - peak_s) / sum_s)
        shifts.append(shard[4:5] / shard[2:3] - mean)
    for d in (2, 1, 3, 0):
        pa = lax.rem(a + d, 4)
        term = acc2[pa]
        total = scales[0] * (term[:, 0:128] + shifts[0] * term[:, 128:256])
        for k in range(3):
            term = rb2[k, pa].astype(F32)
            total += scales[k + 1] * (term[:, 0:128] + shifts[k + 1] * term[:, 128:256])
        if d:
            sb3[d - 1] = total.astype(BF16)
            go(sb3.at[d - 1], rb3.at[d - 1], R3 + d - 1, plane_dev(d, 0))
    for d in (1, 3, 2):
        arrive(rb3.at[d - 1], R3 + d - 1)
        total += rb3[d - 1].astype(F32)
    total = total.astype(BF16)

    place[...] = jnp.zeros_like(place)
    for k in range(4):
        place[k, 32 * k:32 * k + 32] = total[128:160]
    nt = (((1,), (1,)), ((), ()))
    spread_out = lax.dot_general(un1[...], total[0:128], nt, preferred_element_type=F32)
    for k in range(4):
        spread_out += lax.dot_general(un2[k], place[k], nt, preferred_element_type=F32)
    sb4[...] = spread_out.astype(BF16).reshape(16, 16, 128)
    rb4[z] = sb4[z]
    for n, d in enumerate(Z_ORDER):
        go(sb4.at[lax.rem(z + d, 16)], rb4.at[z], ZR + n, z_dev(d))
    for n, d in enumerate(Z_ORDER):
        arrive(rb4.at[lax.rem(z + 16 - d, 16)], ZR + n)
    full = jnp.sum(rb4[...].astype(F32), axis=0)
    sb5[c] = full
    go(sb5.at[c], sb5.at[c], SIB_R5, sibling)
    arrive(sb5.at[o], SIB_R5)
    grads = []
    for h in range(2):
        block = sb5[h]
        for row in range(12):
            at = 32 * (row % 4)
            tail[h, row:row + 1, 0:32] = block[12 + row // 4:13 + row // 4, at:at + 32]
        grads.append(jnp.where(c == 0, block[0:6], block[6:12]))
        grads.append(jnp.where(c == 0, tail[h, 0:6], tail[h, 6:12])[:, 0:32])
    grad_ref[:, 0:128] = grads[0]
    grad_ref[:, 128:160] = grads[1]
    grad_ref[:, 160:288] = grads[2]
    grad_ref[:, 288:320] = grads[3]
    for copy in pending:
        copy.wait_send()


def on_device(
    student_hidden, teacher_hidden, student_head, teacher_head,
    teacher_row, live_counts, branch_id, branch_ratio,
):
    vmem = pl.BlockSpec(memory_space=pltpu.VMEM)
    hbm = pl.BlockSpec(memory_space=pl.ANY)
    loss, grad = pl.pallas_call(
        kernel,
        out_shape=(
            jax.ShapeDtypeStruct((1, 128), F32),
            jax.ShapeDtypeStruct((6, 320), F32),
        ),
        in_specs=[hbm] * 8,
        out_specs=(vmem, vmem),
        scratch_shapes=[
            pltpu.VMEM((6, 320), BF16),
            pltpu.VMEM((6, 256), BF16),
            pltpu.VMEM((1, 192), jnp.int32),
            pltpu.VMEM((1, 32), jnp.int32),
            pltpu.VMEM((1, 192), jnp.int32),
            pltpu.VMEM((1, 16), F32),
            pltpu.VMEM((280, 5120), BF16),
            pltpu.VMEM((280, 4096), BF16),
            pltpu.VMEM((2, 16, 160, 280), BF16),
            pltpu.VMEM((16, 160, 280), BF16),
            pltpu.VMEM((8, 384), F32),
            pltpu.VMEM((2, 16, 128), BF16),
            pltpu.VMEM((16, 2, 16, 128), BF16),
            pltpu.VMEM((3, LIVE, 512), BF16),
            pltpu.VMEM((2, 16, HALF, 128), BF16),
            pltpu.VMEM((256, 128), BF16),
            pltpu.VMEM((4, 256, 128), BF16),
            pltpu.VMEM((2, 8, 128), F32),
            pltpu.VMEM((16, 8, 128), F32),
            pltpu.VMEM((16, 8, 128), F32),
            pltpu.VMEM((2, 288, 256), BF16),
            pltpu.VMEM((3, 4, 160, 256), BF16),
            pltpu.VMEM((3, 4, 160, 256), BF16),
            pltpu.VMEM((4, 160, 256), F32),
            pltpu.VMEM((3, 160, 128), BF16),
            pltpu.VMEM((3, 160, 128), BF16),
            pltpu.VMEM((4, 128, 128), BF16),
            pltpu.VMEM((16, 16, 128), BF16),
            pltpu.VMEM((16, 16, 128), BF16),
            pltpu.VMEM((2, 16, 128), F32),
            pltpu.VMEM((2, 16, 128), F32),
            pltpu.SemaphoreType.DMA((2,)),
            pltpu.SemaphoreType.DMA((6,)),
            pltpu.SemaphoreType.DMA((N_SEMS,)),
            pltpu.SemaphoreType.DMA((N_SEMS,)),
        ],
        compiler_params=pltpu.CompilerParams(
            collective_id=0, has_side_effects=True, vmem_limit_bytes=60 * 1024 * 1024
        ),
    )(
        student_hidden, teacher_hidden, student_head.T, teacher_head.T,
        teacher_row.reshape(1, -1), live_counts.reshape(1, -1),
        branch_id.reshape(1, -1), branch_ratio.reshape(1, -1),
    )
    return loss[0, 0:6], grad


def solution(mesh):
    in_specs = (
        P("rows", "vocab"),
        P("rows", "vocab"),
        P(None, ("rows", "vocab")),
        P(None, ("rows", "vocab")),
        P(),
        P(),
        P(),
        P(),
    )
    out_specs = (P("rows"), P("rows", "vocab"))
    return jax.shard_map(
        on_device, mesh=mesh, in_specs=in_specs,
        out_specs=out_specs, check_vma=False,
    )
```

time: 94.4 us -> 75.3 us (0.80)
  Pallas kernels: 83.3 us -> 72 us
  local copies, waits for them, and re-layouts: 10.1 us -> 2.44 us
    pallas_call x1, Pallas kernels: 83.3 us -> 72 us  [on_device(): pl.pallas_call(kernel, out_shape=(jax.ShapeDtypeStruct((1, 128), F32), ja...]
    unnamed x15 -> x1, local copies, waits for them, and re-layouts: 9.54 us -> 1.31 us
where the time goes in v2:
time: 75.3 us; the launch traced here: 75.1 us
  Pallas kernels  72 us (96%)
  local copies, waits for them, and re-layouts  2.44 us (3%)
    pallas_call x1, Pallas kernels, on_device(): pl.pallas_call(kernel, out_shape=(jax.ShapeDtypeStruct((1, 128), F32), ja...  72 us

profile of v2, /device:TPU:1, one launch (start us, length us, event | category | flops | bytes accessed | tf_op | source)
XLA Modules:
  0.0 75.1 jit_solution(6886692498978373741)
XLA Ops:
  0.6 72.0 %shard_map.95 = (f32[1,128]{1,0:T(1,128)}, f32[6,320]{1,0:T(8,128)}) custom-call(bf16[6,320]{1,0:T(8,128)(2,1)} %sh_hbm.1, bf16[6,256]{1,0:T(8,128)(2,1)} %th_hbm.1, bf16[280,5120]{1,0:T(8,128)(2,1)} %bitcast.8, bf16[280,4096]{1,0:T(8,128)(2,1)} %bitcast.9, s32[1,192]{1,0:T(1,128)} %bitcast.10, s32[1,32]{1,0:T(1,128)} %bitcast.12, s32[1,192]{1,0:T(1,128)} %bitcast.11, ...), custom_call_target="tpu_custom_call" | custom-call | tf_op jit(solution)/shard_map/pallas_call | solution.py:419
  72.6 1.1 %slice_bitcast_fusion = f32[6]{0:T(128)} fusion(f32[1,128]{1,0:T(1,128)} %get-tuple-element.4), kind=kLoop, calls=%fused_computation | loop fusion | bytes 48 | tf_op jit(solution)/shard_map/squeeze | solution.py:472
  73.8 1.3 %copy.11 = f32[6,320]{1,0:T(8,128)} copy(f32[6,320]{1,0:T(8,128)} %get-tuple-element.9) | data formatting | bytes 15360

commit v3 on v2

--- a/solution.py
+++ b/solution.py
@@ -9,7 +9,7 @@
 F32 = jnp.float32
 BF16 = jnp.bfloat16
 LIVE = 112
-HALF = 288
+HALF = 256
 
 SIB_P, SIB_X, SIB_ST, SIB_W, SIB_G, SIB_R5 = 0, 1, 17, 18, 20, 21
 ZP, ZST, ZR = 22, 37, 52
@@ -60,7 +60,7 @@
     sh_hbm, th_hbm, ws_hbm, wt_hbm, trow_hbm, live_hbm, branch_hbm, ratio_hbm,
     loss_ref, grad_ref,
     sh_ref, th_ref, trow_ref, live_ref, branch_ref, ratio_ref,
-    wst, wtt, wh, wsib, wide, parts, zbuf, sel, xbuf, un1, un2, st_a, st_b, st_c,
+    wst, wtt, wh, wsib, wide, parts, zbuf, sel, xbuf, un, st_a, st_b, st_c,
     g2, sb2, rb2, acc2, sb3, rb3, place, sb4, rb4, sb5, tail,
     head_sem, small_sem, send, recv,
 ):
@@ -147,7 +147,9 @@
         pack_t = jnp.where(row16 == i, th[i:i + 1, 0:128], pack_t)
         pack_t = jnp.where(row16 == 6 + i, th[i:i + 1, 128:256], pack_t)
     for i in range(3):
-        pack_s = jnp.where(row16 == 12 + i, s2[i:i + 1, :] + s2_high[i + 3:i + 4, :], pack_s)
+        both = s2[i:i + 1, :] + s2_high[i + 3:i + 4, :]
+        pack_s = jnp.where(row16 == 12 + i, both, pack_s)
+        pack_t = jnp.where(row16 == 12 + i, both, pack_t)
     parts[0] = pack_s.astype(BF16)
     parts[1] = pack_t.astype(BF16)
     zbuf[z, c] = parts[c]
@@ -172,15 +174,18 @@
         jnp.where(iota((16, 192), 0) == branch_ref[...], ratio_col, 0.0), axis=0, keepdims=True
     )
     weight = as_row(jnp.sum(jnp.where(pick, ratio_of, 0.0), axis=1, keepdims=True), 128)
-    source = jnp.where(c == 0, pos_of, teacher_of).astype(jnp.int32)[0:LIVE]
-    src_owner = sixth(source)
-    src_slot = source - 6 * src_owner
-    src_z = lax.shift_right_logical(src_owner, 1)
-    base = src_z * 32 + jnp.bitwise_and(src_owner, 1) * 16
-    low = src_slot < 3
+    def origin(source):
+        owner = sixth(source)
+        at_z = lax.shift_right_logical(owner, 1)
+        return at_z * 32 + jnp.bitwise_and(owner, 1) * 16, source - 6 * owner
+
+    pos_of = pos_of.astype(jnp.int32)[0:LIVE]
+    base, src_slot = origin(jnp.where(c == 0, pos_of, teacher_of.astype(jnp.int32)[0:LIVE]))
+    base_s, slot_s = origin(pos_of)
+    low = slot_s < 3
     column = iota((LIVE, 512), 1)
     for k, at in enumerate((
-        base + src_slot, base + 6 + src_slot, base + 12 + jnp.where(low, src_slot, src_slot - 3)
+        base + src_slot, base + 6 + src_slot, base_s + 12 + jnp.where(low, slot_s, slot_s - 3)
     )):
         sel[k] = jnp.where(column == at, 1.0, 0.0).astype(BF16)
 
@@ -197,9 +202,10 @@
         j = jnp.where(wanted & (slot < count), start + slot, -1.0).astype(jnp.int32)
         return jnp.where(iota((256, 128), 1) == j, 1.0, 0.0).astype(BF16)
 
-    un1[...] = back(q, q < 12)
+    place[...] = jnp.zeros_like(place)
+    un[:, 0:128] = back(q, q < 12)
     for g in range(4):
-        un2[g] = back((q - 12) * 4 + g, (q >= 12) & (q < 15))
+        un[:, 128 * g + 128:128 * g + 256] = back((q - 12) * 4 + g, (q >= 12) & (q < 15))
 
     pl.semaphore_wait(barrier, 31)
     go(parts.at[o], zbuf.at[z, c], SIB_P, sibling)
@@ -207,19 +213,18 @@
     for n, d in enumerate(Z_ORDER):
         go(zbuf.at[z], zbuf.at[z], ZP + n, z_dev(d))
 
-    heads[0].wait()
-    for part in range(2):
+    def turn(part):
         for u in range(4 * part, 4 * part + 4):
             turned = jnp.transpose(wst[:, 640 * u:640 * u + 640])
             for k in range(4):
                 wh[k % 2, 2 * u + k // 2] = turned[160 * k:160 * k + 160]
         where = pl.ds(8 * part, 8)
         go(wh.at[o, where], wsib.at[where], SIB_W + part, sibling)
+
+    heads[0].wait()
+    turn(0)
     for n, d in enumerate(Z_ORDER):
         arrive(zbuf.at[lax.rem(z + 16 - d, 16)], ZP + n)
-    for part in range(2):
-        where = pl.ds(8 * part, 8)
-        arrive(wsib.at[where], SIB_W + part)
     raw = zbuf[...].reshape(512, 128)
     chunk = [jnp.dot(sel[k], raw, preferred_element_type=F32) for k in range(3)]
     turned = pltpu.roll(chunk[2], 64, 1)
@@ -232,7 +237,7 @@
     )
     xbuf[c, v, 0:112] = chunk[0].astype(BF16)
     xbuf[c, v, 112:224] = chunk[1].astype(BF16)
-    xbuf[c, v, 224:288] = packed.astype(BF16)
+    xbuf[c, v, 224:256] = jnp.where(c == 0, packed[0:32], packed[32:64]).astype(BF16)
 
     def spread(pa, n):
         block = xbuf.at[c, v_of(pa, b)]
@@ -244,53 +249,76 @@
     for k, d in enumerate((1, 3, 2)):
         go(mine, mine, PA + k, plane_dev(d, 0))
     spread(a, 0)
+    turn(1)
     for k, d in enumerate((1, 3, 2)):
         pa = lax.rem(a + 4 - d, 4)
         arrive(xbuf.at[c, v_of(pa, b)], PA + k)
         spread(pa, k + 1)
-    for n, d0 in enumerate((0, 1, 3, 2)):
+    heads[1].wait()
+    nt = (((1,), (1,)), ((), ()))
+    student = jnp.zeros((280, LIVE), F32)
+    teacher = jnp.zeros((280, LIVE), F32)
+
+    def rows_of(part, w):
+        return jnp.concatenate([xbuf[part, w, 0:112], xbuf[part, w, 112:224]], axis=1)
+
+    def come(n, d0):
         for k, d in enumerate((2, 1, 3)):
             block = xbuf.at[c, v_of(lax.rem(a + 4 - d0, 4), lax.rem(b + 4 - d, 4))]
             arrive(block, PB + 3 * n + k)
             go(block, block, SIB_X + 4 + 3 * n + k, sibling)
-    for n, d0 in enumerate((0, 1, 3, 2)):
+
+    def come_over(n, d0):
         pa = lax.rem(b + 4 - d0, 4)
         arrive(xbuf.at[o, v_sib(pa, a)], SIB_X + n)
-    for n, d0 in enumerate((0, 1, 3, 2)):
         for k, d in enumerate((2, 1, 3)):
-            pa, pb = lax.rem(b + 4 - d0, 4), lax.rem(a + 4 - d, 4)
-            arrive(xbuf.at[o, v_sib(pa, pb)], SIB_X + 4 + 3 * n + k)
-    heads[1].wait()
-
-    nt = (((1,), (1,)), ((), ()))
+            arrive(xbuf.at[o, v_sib(pa, lax.rem(a + 4 - d, 4))], SIB_X + 4 + 3 * n + k)
+
+    def logits_of(student, teacher, d0):
+        at = lax.rem(x + 4 - d0, 4)
+        left = [
+            wst[:, pl.ds(pl.multiple_of(1280 * at + begin, 128), 256)] for begin in (0, 384, 640, 1024)
+        ]
+        right = [rows_of(0, 4 * at + k) for k in range(4)]
+        student += lax.dot_general(
+            jnp.concatenate(left, axis=1), jnp.concatenate(right, axis=1), nt,
+            preferred_element_type=F32,
+        )
+        at = lax.rem(y + 4 - d0, 4)
+        left = [wtt[:, pl.ds(pl.multiple_of(1024 * k + 256 * at, 128), 256)] for k in range(4)]
+        right = [rows_of(1, 4 * k + at) for k in range(4)]
+        teacher += lax.dot_general(
+            jnp.concatenate(left, axis=1), jnp.concatenate(right, axis=1), nt,
+            preferred_element_type=F32,
+        )
+        return student, teacher
+
+    places = (0, 1, 3, 2)
+    for n, d0 in enumerate(places):
+        come(n, d0)
+        if n:
+            come_over(n - 1, places[n - 1])
+            student, teacher = logits_of(student, teacher, places[n - 1])
+    come_over(3, places[3])
+    for part in range(2):
+        where = pl.ds(8 * part, 8)
+        arrive(wsib.at[where], SIB_W + part)
+    student, teacher = logits_of(student, teacher, places[3])
     lane = iota((64, 128), 1)
-    student = jnp.zeros((280, LIVE), F32)
-    teacher = jnp.zeros((280, LIVE), F32)
-    for u in range(8):
-        even, odd_ = 2 * u, 2 * u + 1
-        first, second = xbuf[0, even, 224:288].astype(F32), xbuf[0, odd_, 224:288].astype(F32)
-        top = jnp.where(lane < 64, first, second)
-        rest = pltpu.roll(jnp.where(lane < 64, second, first), 64, 1)[16:64]
-        block = jnp.concatenate(
-            [
-                xbuf[0, even, 0:112], xbuf[0, even, 112:224],
-                jnp.concatenate([top, rest], axis=0).astype(BF16),
-                xbuf[0, odd_, 0:112], xbuf[0, odd_, 112:224],
-            ],
-            axis=1,
-        )
+    for part in range(2):
+        left, right = [], []
+        for u in range(4 * part, 4 * part + 4):
+            first, second = [
+                jnp.concatenate([xbuf[0, w, 224:256], xbuf[1, w, 224:256]], axis=0).astype(F32)
+                for w in (2 * u, 2 * u + 1)
+            ]
+            top = jnp.where(lane < 64, first, second)
+            rest = pltpu.roll(jnp.where(lane < 64, second, first), 64, 1)[16:64]
+            left.append(wst[:, 640 * u + 256:640 * u + 384])
+            right.append(jnp.concatenate([top, rest], axis=0).astype(BF16))
         student += lax.dot_general(
-            wst[:, 640 * u:640 * u + 640], block, nt, preferred_element_type=F32
-        )
-        block = jnp.concatenate(
-            [
-                xbuf[1, even, 0:112], xbuf[1, even, 112:224],
-                xbuf[1, odd_, 0:112], xbuf[1, odd_, 112:224],
-            ],
-            axis=1,
-        )
-        teacher += lax.dot_general(
-            wtt[:, 512 * u:512 * u + 512], block, nt, preferred_element_type=F32
+            jnp.concatenate(left, axis=1), jnp.concatenate(right, axis=1), nt,
+            preferred_element_type=F32,
         )
     zeros = jnp.zeros((280, 128 - LIVE), F32)
     student = jnp.concatenate([student, zeros], axis=1)
@@ -309,26 +337,29 @@
     go(st_a.at[c], st_a.at[c], SIB_ST, sibling)
     arrive(st_a.at[o], SIB_ST)
     chip = merge(st_a[...])
-    put_stats(st_b.at[v], chip)
-    for n, (da, db) in enumerate(plane):
-        go(st_b.at[v], st_b.at[v], PST + n, plane_dev(da, db))
-
     mass = expo * jnp.exp(peak_s - chip[0])
     g2[c, 0:280, 0:128] = (mass * (diff - chip[4] / chip[2])).astype(BF16)
     g2[c, 0:280, 128:256] = mass.astype(BF16)
     go(g2.at[c], g2.at[c], SIB_G, sibling)
+    put_stats(st_b.at[v], chip)
+    for n, (da, db) in enumerate(plane):
+        go(st_b.at[v], st_b.at[v], PST + n, plane_dev(da, db))
     arrive(g2.at[o], SIB_G)
 
     def products(d):
-        pb = lax.rem(b + d, 4)
-        for pa in range(4):
-            w = v_of(pa, pb)
-            total = jnp.dot(wh[c, w], g2[c, 0:280], preferred_element_type=F32)
-            total += jnp.dot(wsib[w], g2[o, 0:280], preferred_element_type=F32)
-            if d:
-                sb2[d - 1, pa] = total.astype(BF16)
-            else:
-                acc2[pa] = total
+        places_here = [v_of(pa, lax.rem(b + d, 4)) for pa in range(4)]
+        total = jnp.dot(
+            jnp.concatenate([wh[c, w] for w in places_here], axis=0), g2[c, 0:280],
+            preferred_element_type=F32,
+        )
+        total += jnp.dot(
+            jnp.concatenate([wsib[w] for w in places_here], axis=0), g2[o, 0:280],
+            preferred_element_type=F32,
+        )
+        if d:
+            sb2[d - 1] = total.astype(BF16).reshape(4, 160, 256)
+        else:
+            acc2[...] = total.reshape(4, 160, 256)
 
     for d in (2, 1, 3):
         products(d)
@@ -377,13 +408,10 @@
         total += rb3[d - 1].astype(F32)
     total = total.astype(BF16)
 
-    place[...] = jnp.zeros_like(place)
+    place[:, 0:128] = total[0:128]
     for k in range(4):
-        place[k, 32 * k:32 * k + 32] = total[128:160]
-    nt = (((1,), (1,)), ((), ()))
-    spread_out = lax.dot_general(un1[...], total[0:128], nt, preferred_element_type=F32)
-    for k in range(4):
-        spread_out += lax.dot_general(un2[k], place[k], nt, preferred_element_type=F32)
+        place[32 * k:32 * k + 32, 128 * k + 128:128 * k + 256] = total[128:160]
+    spread_out = lax.dot_general(un[...], place[...], nt, preferred_element_type=F32)
     sb4[...] = spread_out.astype(BF16).reshape(16, 16, 128)
     rb4[z] = sb4[z]
     for n, d in enumerate(Z_ORDER):
@@ -393,13 +421,18 @@
     full = jnp.sum(rb4[...].astype(F32), axis=0)
     sb5[c] = full
     go(sb5.at[c], sb5.at[c], SIB_R5, sibling)
+
+    def ends(h, block):
+        for row in range(12):
+            at = 32 * (row % 4)
+            tail[h, row:row + 1, 0:32] = block[12 + row // 4:13 + row // 4, at:at + 32]
+
+    ends(c, full)
     arrive(sb5.at[o], SIB_R5)
+    ends(o, sb5[o])
     grads = []
     for h in range(2):
         block = sb5[h]
-        for row in range(12):
-            at = 32 * (row % 4)
-            tail[h, row:row + 1, 0:32] = block[12 + row // 4:13 + row // 4, at:at + 32]
         grads.append(jnp.where(c == 0, block[0:6], block[6:12]))
         grads.append(jnp.where(c == 0, tail[h, 0:6], tail[h, 6:12])[:, 0:32])
     grad_ref[:, 0:128] = grads[0]
@@ -440,8 +473,7 @@
             pltpu.VMEM((16, 2, 16, 128), BF16),
             pltpu.VMEM((3, LIVE, 512), BF16),
             pltpu.VMEM((2, 16, HALF, 128), BF16),
-            pltpu.VMEM((256, 128), BF16),
-            pltpu.VMEM((4, 256, 128), BF16),
+            pltpu.VMEM((256, 640), BF16),
             pltpu.VMEM((2, 8, 128), F32),
             pltpu.VMEM((16, 8, 128), F32),
             pltpu.VMEM((16, 8, 128), F32),
@@ -451,7 +483,7 @@
             pltpu.VMEM((4, 160, 256), F32),
             pltpu.VMEM((3, 160, 128), BF16),
             pltpu.VMEM((3, 160, 128), BF16),
-            pltpu.VMEM((4, 128, 128), BF16),
+            pltpu.VMEM((128, 640), BF16),
             pltpu.VMEM((16, 16, 128), BF16),
             pltpu.VMEM((16, 16, 128), BF16),
             pltpu.VMEM((2, 16, 128), F32),

time: 75.3 us -> 73.9 us (0.981)
  Pallas kernels: 72 us -> 70.5 us
    pallas_call x1, Pallas kernels: 72 us -> 70.5 us  [on_device(): pl.pallas_call(kernel, out_shape=(jax.ShapeDtypeStruct((1, 128), F32), ja...]
where the time goes in v3:
time: 73.9 us; the launch traced here: 73.6 us
  Pallas kernels  70.5 us (95%)
  local copies, waits for them, and re-layouts  2.44 us (3%)
    pallas_call x1, Pallas kernels, on_device(): pl.pallas_call(kernel, out_shape=(jax.ShapeDtypeStruct((1, 128), F32), ja...  70.5 us

profile of v3, /device:TPU:1, one launch (start us, length us, event | category | flops | bytes accessed | tf_op | source)
XLA Modules:
  0.0 73.6 jit_solution(14643870191934393238)
XLA Ops:
  0.6 70.5 %shard_map.95 = (f32[1,128]{1,0:T(1,128)}, f32[6,320]{1,0:T(8,128)}) custom-call(bf16[6,320]{1,0:T(8,128)(2,1)} %sh_hbm.1, bf16[6,256]{1,0:T(8,128)(2,1)} %th_hbm.1, bf16[280,5120]{1,0:T(8,128)(2,1)} %bitcast.8, bf16[280,4096]{1,0:T(8,128)(2,1)} %bitcast.9, s32[1,192]{1,0:T(1,128)} %bitcast.10, s32[1,32]{1,0:T(1,128)} %bitcast.12, s32[1,192]{1,0:T(1,128)} %bitcast.11, ...), custom_call_target="tpu_custom_call" | custom-call | tf_op jit(solution)/shard_map/pallas_call | solution.py:452
  71.2 1.1 %slice_bitcast_fusion = f32[6]{0:T(128)} fusion(f32[1,128]{1,0:T(1,128)} %get-tuple-element.4), kind=kLoop, calls=%fused_computation | loop fusion | bytes 48 | tf_op jit(solution)/shard_map/squeeze | solution.py:504
  72.3 1.3 %copy.11 = f32[6,320]{1,0:T(8,128)} copy(f32[6,320]{1,0:T(8,128)} %get-tuple-element.9) | data formatting | bytes 15360

commit v4 on v3

--- a/solution.py
+++ b/solution.py
@@ -386,7 +386,7 @@
     at = jnp.where(slot < count, start + slot, -1.0).astype(jnp.int32)
     loss_ref[...] = jnp.sum(
         jnp.where(iota((128, 128), 0) == at, loss, 0.0), axis=0, keepdims=True
-    )
+    )[:, 0:6]
     mean = cross / sum_s
     scales, shifts = [], []
     for d in range(4):
@@ -443,6 +443,17 @@
         copy.wait_send()
 
 
+def hand_out(loss_in, grad_in, loss_ref, grad_ref, sem):
+    copies = [
+        pltpu.make_async_copy(loss_in, loss_ref, sem.at[0]),
+        pltpu.make_async_copy(grad_in, grad_ref, sem.at[1]),
+    ]
+    for copy in copies:
+        copy.start()
+    for copy in copies:
+        copy.wait()
+
+
 def on_device(
     student_hidden, teacher_hidden, student_head, teacher_head,
     teacher_row, live_counts, branch_id, branch_ratio,
@@ -452,7 +463,7 @@
     loss, grad = pl.pallas_call(
         kernel,
         out_shape=(
-            jax.ShapeDtypeStruct((1, 128), F32),
+            jax.ShapeDtypeStruct((1, 6), F32),
             jax.ShapeDtypeStruct((6, 320), F32),
         ),
         in_specs=[hbm] * 8,
@@ -501,7 +512,18 @@
         teacher_row.reshape(1, -1), live_counts.reshape(1, -1),
         branch_id.reshape(1, -1), branch_ratio.reshape(1, -1),
     )
-    return loss[0, 0:6], grad
+    loss, grad = pl.pallas_call(
+        hand_out,
+        out_shape=(
+            jax.ShapeDtypeStruct((1, 6), F32),
+            jax.ShapeDtypeStruct((6, 320), F32),
+        ),
+        in_specs=[hbm, hbm],
+        out_specs=(hbm, hbm),
+        scratch_shapes=[pltpu.SemaphoreType.DMA((2,))],
+        compiler_params=pltpu.CompilerParams(vmem_limit_bytes=60 * 1024 * 1024),
+    )(loss, grad)
+    return loss.reshape(6), grad
 
 
 def solution(mesh):

time: 73.9 us -> 72.8 us (0.985)
  local copies, waits for them, and re-layouts: 2.44 us -> 0 us
  Pallas kernels: 70.5 us -> 72 us
    pallas_call x1 -> x2, Pallas kernels: 70.5 us -> 72 us  [the longest x1 70.5 us: on_device(): pl.pallas_call(kernel, out_shape=(jax.ShapeDtypeStruct((1, 6), F32), jax....]
    unnamed x1 -> x0, local copies, waits for them, and re-layouts: 1.31 us -> none
    squeeze x1 -> x0, local copies, waits for them, and re-layouts: 1.14 us -> none  [on_device(): return (loss[0, 0:6], grad)]
where the time goes in v4:
time: 72.8 us; the launch traced here: 72.7 us
  Pallas kernels  72 us (99%)
    pallas_call x1, Pallas kernels, on_device(): pl.pallas_call(kernel, out_shape=(jax.ShapeDtypeStruct((1, 6), F32), jax....  70.5 us
    pallas_call x1, Pallas kernels, on_device(): pl.pallas_call(hand_out, out_shape=(jax.ShapeDtypeStruct((1, 6), F32), ja...  1.51 us

profile of v4, /device:TPU:1, one launch (start us, length us, event | category | flops | bytes accessed | tf_op | source)
XLA Modules:
  0.0 72.7 jit_solution(11227757256221368165)
XLA Ops:
  0.6 70.5 %shard_map.95 = (f32[1,6]{1,0:T(1,128)}, f32[6,320]{1,0:T(8,128)}) custom-call(bf16[6,320]{1,0:T(8,128)(2,1)} %sh_hbm.1, bf16[6,256]{1,0:T(8,128)(2,1)} %th_hbm.1, bf16[280,5120]{1,0:T(8,128)(2,1)} %bitcast.7, bf16[280,4096]{1,0:T(8,128)(2,1)} %bitcast.8, s32[1,192]{1,0:T(1,128)} %bitcast.9, s32[1,32]{1,0:T(1,128)} %bitcast.11, s32[1,192]{1,0:T(1,128)} %bitcast.10, ...), custom_call_target="tpu_custom_call" | custom-call | tf_op jit(solution)/shard_map/pallas_call | solution.py:463
  71.2 1.5 %shard_map.96 = (f32[1,6]{1,0:T(1,128)}, f32[6,320]{1,0:T(8,128)}) custom-call(f32[1,6]{1,0:T(1,128)} %get-tuple-element.6.loss_in, f32[6,320]{1,0:T(8,128)} %get-tuple-element.7.grad_in), custom_call_target="tpu_custom_call" | custom-call | tf_op jit(solution)/shard_map/pallas_call | solution.py:515

commit v5 on v4

--- a/solution.py
+++ b/solution.py
@@ -338,6 +338,7 @@
     arrive(st_a.at[o], SIB_ST)
     chip = merge(st_a[...])
     mass = expo * jnp.exp(peak_s - chip[0])
+    g2[c, 272:288] = jnp.zeros((16, 256), BF16)
     g2[c, 0:280, 0:128] = (mass * (diff - chip[4] / chip[2])).astype(BF16)
     g2[c, 0:280, 128:256] = mass.astype(BF16)
     go(g2.at[c], g2.at[c], SIB_G, sibling)

time: 72.8 us -> 72.8 us (level)
  no operation moved by 1% of the time
where the time goes in v5:
time: 72.8 us; the launch traced here: 72.7 us
  Pallas kernels  72 us (99%)
    pallas_call x1, Pallas kernels, on_device(): pl.pallas_call(kernel, out_shape=(jax.ShapeDtypeStruct((1, 6), F32), jax....  70.5 us
    pallas_call x1, Pallas kernels, on_device(): pl.pallas_call(hand_out, out_shape=(jax.ShapeDtypeStruct((1, 6), F32), ja...  1.51 us

profile of v5, /device:TPU:1, one launch (start us, length us, event | category | flops | bytes accessed | tf_op | source)
XLA Modules:
  0.0 72.7 jit_solution(11684659071257900164)
XLA Ops:
  0.6 70.5 %shard_map.95 = (f32[1,6]{1,0:T(1,128)}, f32[6,320]{1,0:T(8,128)}) custom-call(bf16[6,320]{1,0:T(8,128)(2,1)} %sh_hbm.1, bf16[6,256]{1,0:T(8,128)(2,1)} %th_hbm.1, bf16[280,5120]{1,0:T(8,128)(2,1)} %bitcast.7, bf16[280,4096]{1,0:T(8,128)(2,1)} %bitcast.8, s32[1,192]{1,0:T(1,128)} %bitcast.9, s32[1,32]{1,0:T(1,128)} %bitcast.11, s32[1,192]{1,0:T(1,128)} %bitcast.10, ...), custom_call_target="tpu_custom_call" | custom-call | tf_op jit(solution)/shard_map/pallas_call | solution.py:464
  71.2 1.5 %shard_map.96 = (f32[1,6]{1,0:T(1,128)}, f32[6,320]{1,0:T(8,128)}) custom-call(f32[1,6]{1,0:T(1,128)} %get-tuple-element.6.loss_in, f32[6,320]{1,0:T(8,128)} %get-tuple-element.7.grad_in), custom_call_target="tpu_custom_call" | custom-call | tf_op jit(solution)/shard_map/pallas_call | solution.py:516
